TPU v7x, 256 devices: a whole 4x4x8 slice. The times are simulated.
256 devices in a mesh: dom: 64 (over z, x, core), sub: 4 (over y).
Axes of the slice: x: 4, y: 4, z: 8, core: 2. Of those that a mesh axis runs over, the one named last changes fastest.
Arguments:
- unknowns: float32 [9, 35, 65536], P(None, None, ('dom', 'sub')), may hold values from -6 to 6
- gradients: float32 [3, 3, 65536], P(None, None, ('dom', 'sub')), may hold values from -0.3 to 0.3
- face_normals: float32 [4, 3, 65536], P(None, None, ('dom', 'sub')), may hold values from -0.3 to 0.3
- materials: float32 [3, 65536], P(None, ('dom', 'sub')), may hold values from 0.5 to 2
- live_count: int32 [256], P(('dom', 'sub')), may hold values from 64 to 256, as said below
- neighbour_code: int32 [4, 65536], P(None, ('dom', 'sub')), may hold values from 0 to 1279, as said below
- orientation: int32 [4, 65536], P(None, ('dom', 'sub')), may hold values from 0 to 2
- send_face: int32 [57344], P(('dom', 'sub')), may hold values from 0 to 1023, as said below
- fault_face: int32 [8192], P(('dom', 'sub')), may hold values from 0 to 1023, as said below
- fault_dip: float32 [2, 8192], P(None, ('dom', 'sub')), may hold values from -3.140625 to 3.140625
- cohesion: float32 [15, 8192], P(None, ('dom', 'sub')), may hold values from 0.05 to 1
- stiffness: float32 [3, 35, 35], replicated, may hold values from -1 to 1
- projection: float32 [4, 35, 15], replicated, may hold values from -1 to 1
- lifting: float32 [4, 15, 35], replicated, may hold values from -0.75 to 0.75
- rotations: float32 [3, 15, 15], replicated, may hold values from -1.5 to 1.5
Outputs:
- unknowns_out: float32 [9, 35, 65536], P(None, None, ('dom', 'sub'))
- fault_slip: float32 [3, 15, 8192], P(None, None, ('dom', 'sub'))
Inputs may be any that keep to these rules, and one draw needn't show every extreme that they name: A device's cluster elements are its first live_count slots. A device and the device 64 / 2 further along dom with the same sub index hold at most 320 live elements together; some such pair holds exactly that. `neighbour_code`: values below 1024 name face i' of the device's own element e' as i' * 256 + e'; 1024 + k * 28 + s names slot s of halo block k; 1248 + f names fault slot f. Faces of live elements name only faces of live elements; each halo slot that arrives is named by exactly one face, and fault slot f by the face fault_face[f] alone. `send_face`: on each device, block k of 8 holds 28 codes i * 256 + e of faces of live elements, sent to the device o_k further along dom, o = (1, 2, 3, 4, -1, -2, -3, -4). `fault_face`: on each device, 32 distinct codes i * 256 + e of faces of live elements; slot f faces slot f of the device whose sub index differs in its lowest bit.
All inputs are finite; a program needn't handle non-finite values.
Results may differ from a plain program's by a relative error of at most 0.0003.
Values sent between devices are 32-bit elements; how exact they have to be, the bound alone decides.
A program may use at most 128 MiB of HBM per device.

v0:
```python
import functools

import jax
import jax.numpy as jnp
from jax import lax
from jax.experimental import pallas as pl
from jax.experimental.pallas import tpu as pltpu
from jax.sharding import PartitionSpec as P

STEPS = 2
DEGREES = 4
OFFSETS = (1, 2, 3, 4, -1, -2, -3, -4)
FRICTION = 0.6
HIGHEST = lax.Precision.HIGHEST
MESH = pl.DeviceIdType.MESH

F32 = jnp.float32
BF16 = jnp.bfloat16
Q = 9
B = 35
BP = 40
PTS = 15
PP = 16
E = 256
SLOTS = 256
ROWS = Q * PP


def iota(shape, dim):
    return lax.broadcasted_iota(jnp.int32, shape, dim)


def exact_dot(a, b, dims=(((1,), (0,)), ((), ()))):
    return lax.dot_general(a, b, dims, precision=HIGHEST, preferred_element_type=F32)


def fast_dot(a, b):
    return lax.dot_general(a, b, (((1,), (0,)), ((), ())), preferred_element_type=F32)


def halves(x):
    hi = x.astype(BF16).astype(F32)
    return hi, x - hi


def elastic_rows(s, n, m):
    px, py, pz = s[6] * n[0], s[7] * n[1], s[8] * n[2]
    pressure = m[0] * (px + py + pz)
    return (
        pressure + m[1] * px,
        pressure + m[1] * py,
        pressure + m[1] * pz,
        m[2] * (s[6] * n[1] + s[7] * n[0]),
        m[2] * (s[7] * n[2] + s[8] * n[1]),
        m[2] * (s[6] * n[2] + s[8] * n[0]),
        m[3] * (s[0] * n[0] + s[3] * n[1] + s[5] * n[2]),
        m[3] * (s[3] * n[0] + s[1] * n[1] + s[4] * n[2]),
        m[3] * (s[5] * n[0] + s[4] * n[1] + s[2] * n[2]),
    )


def traction(s, n):
    return (
        s[0] * n[0] + s[3] * n[1] + s[5] * n[2],
        s[3] * n[0] + s[1] * n[1] + s[4] * n[2],
        s[5] * n[0] + s[4] * n[1] + s[2] * n[2],
    )


def kernel(
    n_dom,
    un, gr, fn, mat, live, nc, ori, sf, ff, dip, coh, st, pj, lf, ro,
    out, slip,
    state, cur, integ, R, tr, ths, rt, fx, p1, p2, sp, sg, hs,
    lsf, lpred, lvol, lprj, llift, lrot, coef, fcoef, turn, scoef, fric, slipsum,
    sendb, recvb, sendf, recvf,
    send_sem, recv_sem, fsend_sem, frecv_sem,
):
    me = lax.axis_index("dom")
    sub = lax.axis_index("sub")
    partner = sub + 1 - 2 * (sub % 2)

    barrier = pltpu.get_barrier_semaphore()
    for o in OFFSETS:
        dst = me + o

        @pl.when((dst >= 0) & (dst < n_dom))
        def _():
            pl.semaphore_signal(barrier, inc=1, device_id=(dst, sub), device_id_type=MESH)

    pl.semaphore_signal(barrier, inc=1, device_id=(me, partner), device_id_type=MESH)

    for k, o in enumerate(OFFSETS):
        src = me - o

        @pl.when((src < 0) | (src >= n_dom))
        def _():
            for step in range(STEPS):
                recvb[step, k] = jnp.zeros(recvb.shape[2:], F32)

    rep = (iota((B, 128), 0) == iota((B, 128), 1) % BP) & (iota((B, 128), 1) < 3 * BP)
    rep = jnp.where(rep, 1.0, 0.0)
    low_part = iota((128, 128), 1) >= 2 * BP
    TN = (((0,), (0,)), ((), ()))

    def stacked(x, low):
        hi, lo = halves(x)
        return jnp.where(low, lo, hi).astype(BF16)

    lsf[...] = jnp.zeros_like(lsf)
    for d in range(3):
        lsf[BP * d:BP * d + B, :] = exact_dot(st[d], rep, TN)
    lpred[...] = stacked(lsf[...], low_part)
    for d in range(3):
        lsf[BP * d:BP * d + B, :] = exact_dot(st[d], rep)
    lvol[...] = stacked(lsf[...], low_part)
    lsf[...] = jnp.zeros_like(lsf)
    for i in range(4):
        lsf[PP * i:PP * i + PTS, :] = exact_dot(pj[i], rep, TN)
    lprj[...] = stacked(lsf[0:4 * PP, :], low_part[0:4 * PP])
    total = jnp.zeros((B, 12 * PP), F32)
    for i in range(4):
        place = iota((PTS, 12 * PP), 1) % (4 * PP) == iota((PTS, 12 * PP), 0) + PP * i
        total = total + exact_dot(lf[i], jnp.where(place, 1.0, 0.0), TN)
    total = jnp.concatenate([total, jnp.zeros((48 - B, 12 * PP), F32)], axis=0)
    llift[...] = stacked(total, iota((48, 12 * PP), 1) >= 8 * PP)
    place = jnp.where(iota((PTS, 3 * PP), 1) % PP == iota((PTS, 3 * PP), 0), 1.0, 0.0)
    pad = jnp.zeros((PP - PTS, 3 * PP), F32)
    turns = []
    for h in range(3):
        turns += [exact_dot(ro[h], place, TN), pad]
    lrot[...] = stacked(jnp.concatenate(turns, axis=0), iota((3 * PP, 3 * PP), 1) >= 2 * PP)

    def spread(row):
        return jnp.broadcast_to(row, (8, E))

    lam, mu, rho = mat[0:1, :], mat[1:2, :], mat[2:3, :]
    for d in range(3):
        for c in range(3):
            coef[3 * d + c] = spread(gr[d, c:c + 1, :])
    inv_rho = 1.0 / rho
    for j, row in enumerate((-lam, -2.0 * mu, -mu, -inv_rho)):
        coef[9 + j] = spread(row)
    speed = 0.5 * jnp.sqrt((lam + 2.0 * mu) / rho)
    slip_scale = 1.0 / jnp.sqrt(mu * rho)
    param_blocks = []
    for i in range(4):
        nx, ny, nz = fn[i, 0:1, :], fn[i, 1:2, :], fn[i, 2:3, :]
        cw = speed * jnp.sqrt(nx * nx + ny * ny + nz * nz)
        rows = [0.5 * nx, 0.5 * ny, 0.5 * nz, cw]
        for j, row in enumerate(rows):
            fcoef[i, j] = spread(row)
        h = ori[i:i + 1, :]
        masks = [jnp.where(h == t, 1.0, 0.0) for t in range(3)]
        turn[i, 0] = spread(masks[0])
        turn[i, 1] = spread(masks[1])
        rows += [-lam, -2.0 * mu, -mu, -inv_rho, slip_scale, masks[0], masks[1], masks[2]]
        which = iota((PP, E), 0)
        block = jnp.zeros((PP, E), F32)
        for j, row in enumerate(rows):
            block = jnp.where(which == j, jnp.broadcast_to(row, (PP, E)), block)
        param_blocks.append(block)

    place_h = jnp.where(
        ((iota((224, SLOTS), 1) & 31) < 28)
        & (iota((224, SLOTS), 0) == 28 * (iota((224, SLOTS), 1) >> 5) + (iota((224, SLOTS), 1) & 31)),
        1.0, 0.0,
    )
    place_f = jnp.where(
        ((iota((32, SLOTS), 1) & 31) >= 28)
        & (iota((32, SLOTS), 0) == 4 * (iota((32, SLOTS), 1) >> 5) + (iota((32, SLOTS), 1) & 31) - 28),
        1.0, 0.0,
    )
    codes = exact_dot(jnp.broadcast_to(sf[...].astype(F32), (8, 224)), place_h)
    codes = codes + exact_dot(jnp.broadcast_to(ff[...].astype(F32), (8, 32)), place_f)
    codes = (codes[0:1, :] + 0.5).astype(jnp.int32)
    for i in range(4):
        sp[E * i:E * i + E, :] = jnp.where(iota((E, SLOTS), 0) + E * i == codes, 1.0, 0.0).astype(BF16)

    slot_params = jnp.zeros((3 * PP, SLOTS), F32)
    for i in range(4):
        code = nc[i:i + 1, :]
        for j in range(4):
            p1[i, E * j:E * j + E, :] = jnp.where(iota((E, E), 0) + E * j == code, 1.0, 0.0).astype(BF16)
        halo = code - 1024
        block = jnp.zeros_like(halo)
        for m in range(1, 8):
            block = block + jnp.where(halo >= 28 * m, 1, 0)
        fault = code - 1248
        spot = jnp.where(fault >= 0, fault + 28 * (fault >> 2) + 28, jnp.where(halo >= 0, halo + 4 * block, -1))
        hot = jnp.where(iota((SLOTS, E), 0) == spot, 1.0, 0.0).astype(BF16)
        p2[i] = hot
        hi, rest = halves(param_blocks[i])
        mid, lo = halves(rest)
        left = jnp.concatenate([hi, mid, lo], axis=0).astype(BF16)
        slot_params = slot_params + lax.dot_general(
            left, hot, (((1,), (1,)), ((), ())), preferred_element_type=F32
        )
    slot_params = slot_params[0:PP] + slot_params[PP:2 * PP] + slot_params[2 * PP:3 * PP]
    for j in range(12):
        scoef[j] = spread(slot_params[j:j + 1, :])

    on_fault = (iota((PP, SLOTS), 1) & 31) >= 28
    angles = exact_dot(dip[...], place_f)
    polar, azimuth = angles[0:1, :], angles[1:2, :]
    fric[0] = jnp.broadcast_to(jnp.sin(polar) * jnp.cos(azimuth), (PP, SLOTS))
    fric[1] = jnp.broadcast_to(jnp.sin(polar) * jnp.sin(azimuth), (PP, SLOTS))
    fric[2] = jnp.broadcast_to(jnp.cos(polar), (PP, SLOTS))
    held = jnp.concatenate([exact_dot(coh[...], place_f), jnp.zeros((PP - PTS, SLOTS), F32)], axis=0)
    fric[3] = jnp.where(on_fault & (iota((PP, SLOTS), 0) < PTS), held, 1.0)
    slipsum[...] = jnp.zeros_like(slipsum)

    for q in range(Q):
        state[q] = jnp.concatenate([un[q], jnp.zeros((BP - B, E), F32)], axis=0)
    live_lane = iota((1, E), 1) < live[0]

    def split_modes(x):
        hi, lo = halves(x)
        return jnp.concatenate([hi, lo, hi, jnp.zeros((8, E), F32)], axis=0).astype(BF16)

    def sum_elastic(store):
        def body(rb, carry):
            def get(q, d):
                return R[q, pl.ds(pl.multiple_of(BP * d + 8 * rb, 8), 8), :]

            g = [[coef[3 * d + c] for c in range(3)] for d in range(3)]
            m = [coef[9 + j] for j in range(4)]
            grad = {}
            for i in range(3):
                v = [get(6 + i, d) for d in range(3)]
                for c in range(3):
                    grad[i, c] = v[0] * g[0][c] + v[1] * g[1][c] + v[2] * g[2][c]
            pressure = m[0] * (grad[0, 0] + grad[1, 1] + grad[2, 2])
            res = [
                pressure + m[1] * grad[0, 0],
                pressure + m[1] * grad[1, 1],
                pressure + m[1] * grad[2, 2],
                m[2] * (grad[0, 1] + grad[1, 0]),
                m[2] * (grad[1, 2] + grad[2, 1]),
                m[2] * (grad[0, 2] + grad[2, 0]),
            ]
            for kinds in ((0, 3, 5), (3, 1, 4), (5, 4, 2)):
                force = None
                for c, q in enumerate(kinds):
                    for d in range(3):
                        term = get(q, d) * g[d][c]
                        force = term if force is None else force + term
                res.append(m[3] * force)
            store(pl.ds(pl.multiple_of(8 * rb, 8), 8), res)
            return carry

        lax.fori_loop(0, BP // 8, body, 0, unroll=True)

    def send(step, k):
        return pltpu.make_async_remote_copy(
            src_ref=sendb.at[step, k],
            dst_ref=recvb.at[step, k],
            send_sem=send_sem.at[step, k],
            recv_sem=recv_sem.at[step, k],
            device_id=(me + OFFSETS[k], sub),
            device_id_type=MESH,
        )

    def send_fault(step):
        return pltpu.make_async_remote_copy(
            src_ref=sendf.at[step],
            dst_ref=recvf.at[step],
            send_sem=fsend_sem.at[step],
            recv_sem=frecv_sem.at[step],
            device_id=(me, partner),
            device_id_type=MESH,
        )

    def update(step, carry):
        factor = 1.0
        for degree in range(1, DEGREES + 1):
            source = state if degree == 1 else cur
            for q in range(Q):
                R[q] = fast_dot(lpred[...], split_modes(source[q]))
            factor = factor / (degree + 1)
            base = state if degree == 1 else integ

            def store(rows, res, factor=factor, base=base):
                for q in range(Q):
                    cur[q, rows, :] = res[q]
                    integ[q, rows, :] = base[q, rows, :] + factor * res[q]

            sum_elastic(store)

        for q in range(Q):
            t = fast_dot(lprj[...], split_modes(integ[q]))
            tr[q] = t
            hi, lo = halves(t)
            hi = hi.astype(BF16)
            lo = lo.astype(BF16)
            for i in range(4):
                ths[PP * q:PP * q + PP, E * i:E * i + E] = hi[PP * i:PP * i + PP]
                ths[ROWS + PP * q:ROWS + PP * q + PP, E * i:E * i + E] = lo[PP * i:PP * i + PP]

        picked = fast_dot(ths[...], sp[...])
        picked = picked[0:ROWS] + picked[ROWS:2 * ROWS]
        sg[...] = picked
        main = jnp.transpose(picked[0:128])
        rest = picked[128:ROWS]
        for k in range(8):
            sendb[step, k, 0:32, :] = main[32 * k:32 * k + 32]
            sendb[step, k, 32:48, :] = rest[:, 128 * (k // 4):128 * (k // 4) + 128]
            sendf[step, 8 * k:8 * k + 8, :] = main[32 * k + 24:32 * k + 32]
        for t in range(2):
            sendf[step, 64 + 16 * t:80 + 16 * t, :] = rest[:, 128 * t:128 * t + 128]

        @pl.when(step == 0)
        def _():
            pl.semaphore_wait(barrier, 1 + jnp.minimum(me, 4) + jnp.minimum(n_dom - 1 - me, 4))

        for k, o in enumerate(OFFSETS):
            dst = me + o

            @pl.when((dst >= 0) & (dst < n_dom))
            def _():
                send(step, k).start()

        send_fault(step).start()

        def own_face(i, c):
            g = fast_dot(ths[...], p1[i]).astype(BF16)
            m0, m1 = turn[i, 0] > 0.5, turn[i, 1] > 0.5
            for q in range(Q):
                hi = g[PP * q:PP * q + PP]
                lo = g[ROWS + PP * q:ROWS + PP * q + PP]
                r = fast_dot(lrot[...], jnp.concatenate([hi, lo, hi], axis=0))
                for half in range(2):
                    a = 8 * half
                    rt[q, pl.ds(pl.multiple_of(PP * i + a, 8), 8), :] = jnp.where(
                        m0, r[a:a + 8], jnp.where(m1, r[PP + a:PP + a + 8], r[2 * PP + a:2 * PP + a + 8])
                    )
            m = [coef[9 + j] for j in range(4)]
            n = [fcoef[i, j] for j in range(3)]
            cw = fcoef[i, 3]
            for half in range(2):
                rows = pl.ds(pl.multiple_of(PP * i + 8 * half, 8), 8)
                own = [tr[q, rows, :] for q in range(Q)]
                far = [rt[q, rows, :] for q in range(Q)]
                res = elastic_rows([x + y for x, y in zip(own, far)], n, m)
                for q in range(Q):
                    fx[q, rows, :] = res[q] + cw * (own[q] - far[q])
            return c

        lax.fori_loop(0, 4, own_face, 0, unroll=True)

        for q in range(Q):
            R[q] = fast_dot(lvol[...], split_modes(integ[q]))

        def store_volume(rows, res):
            for q in range(Q):
                cur[q, rows, :] = state[q, rows, :] + res[q]

        sum_elastic(store_volume)
        for q in range(Q):
            hi, lo = halves(fx[q])
            lifted = fast_dot(llift[...], jnp.concatenate([hi, lo, hi], axis=0).astype(BF16))
            cur[q] = cur[q] - lifted[0:BP]

        for k, o in enumerate(OFFSETS):
            src = me - o

            @pl.when((src >= 0) & (src < n_dom))
            def _():
                send(step, k).wait_recv()

        send_fault(step).wait_recv()
        blocks = []
        lower = iota((8, 128), 0) >= 4
        for k in range(8):
            blocks.append(recvb[step, k, 0:24, :])
            blocks.append(jnp.where(lower, recvf[step, 8 * k:8 * k + 8, :], recvb[step, k, 24:32, :]))
        main = jnp.transpose(jnp.concatenate(blocks, axis=0))
        lane = iota((PP, 128), 1)
        tails = []
        for t in range(2):
            tail = recvb[step, 4 * t, 32:48, :]
            for j in range(1, 4):
                tail = jnp.where((lane >> 5) == j, recvb[step, 4 * t + j, 32:48, :], tail)
            tails.append(jnp.where((lane & 31) >= 28, recvf[step, 64 + 16 * t:80 + 16 * t, :], tail))
        tail = jnp.concatenate(tails, axis=1)

        far = []
        m0 = jnp.concatenate([scoef[9], scoef[9]], axis=0) > 0.5
        m1 = jnp.concatenate([scoef[10], scoef[10]], axis=0) > 0.5
        for q in range(Q):
            x = main[PP * q:PP * q + PP] if q < 8 else tail
            hi, lo = halves(x)
            r = fast_dot(lrot[...], jnp.concatenate([hi, lo, hi], axis=0).astype(BF16))
            far.append(jnp.where(m0, r[0:PP], jnp.where(m1, r[PP:2 * PP], r[2 * PP:3 * PP])))

        def double(j):
            return jnp.concatenate([scoef[j], scoef[j]], axis=0)

        n = [double(j) for j in range(3)]
        cw = double(3)
        m = [double(4 + j) for j in range(4)]
        flux = elastic_rows(far, n, m)
        flux = [flux[q] - cw * far[q] for q in range(Q)]

        u = (fric[0], fric[1], fric[2])
        mean = [0.5 * (sg[PP * q:PP * q + PP, :] + far[q]) for q in range(6)]
        force = traction(mean, u)
        along = force[0] * u[0] + force[1] * u[1] + force[2] * u[2]
        tangent = [force[c] - along * u[c] for c in range(3)]
        strength = fric[3] + FRICTION * jnp.maximum(-along, 0.0)
        size = jnp.sqrt(tangent[0] * tangent[0] + tangent[1] * tangent[1] + tangent[2] * tangent[2])
        over = jnp.where(on_fault, 1.0 - strength / jnp.maximum(size, strength), 0.0)
        slip_scale = double(8)
        for c in range(3):
            excess = over * tangent[c]
            flux[6 + c] = flux[6 + c] + excess * m[3]
            slipsum[PP * c:PP * c + PP, :] += excess * slip_scale

        parts = [halves(f) for f in flux]
        left = jnp.concatenate([p[0] for p in parts] + [p[1] for p in parts], axis=0).astype(BF16)
        for i in range(4):
            hs[i] = fast_dot(left, p2[i]).astype(BF16)
        for q in range(Q):
            his = [hs[i, PP * q:PP * q + PP, :] for i in range(4)]
            los = [hs[i, ROWS + PP * q:ROWS + PP * q + PP, :] for i in range(4)]
            lifted = fast_dot(llift[...], jnp.concatenate(his + los + his, axis=0))
            state[q] = jnp.where(live_lane, cur[q] - lifted[0:BP], state[q])

        for k, o in enumerate(OFFSETS):
            dst = me + o

            @pl.when((dst >= 0) & (dst < n_dom))
            def _():
                send(step, k).wait_send()

        send_fault(step).wait_send()
        return carry

    lax.fori_loop(0, STEPS, update, 0)

    for q in range(Q):
        out[q] = state[q, 0:B, :]
    back = jnp.where(
        ((iota((SLOTS, 32), 0) & 31) >= 28)
        & (iota((SLOTS, 32), 1) == 4 * (iota((SLOTS, 32), 0) >> 5) + (iota((SLOTS, 32), 0) & 31) - 28),
        1.0, 0.0,
    )
    gone = exact_dot(slipsum[...], back)
    for c in range(3):
        slip[c] = gone[PP * c:PP * c + PTS]


def on_device(n_dom, *args):
    (un, gr, fn, mat, live, nc, ori, sf, ff, dip, coh, st, pj, lf, ro) = args
    vmem = pl.BlockSpec(memory_space=pltpu.VMEM)
    smem = pl.BlockSpec(memory_space=pltpu.SMEM)

    def f32(*shape):
        return pltpu.VMEM(shape, F32)

    def b16(*shape):
        return pltpu.VMEM(shape, BF16)

    return pl.pallas_call(
        functools.partial(kernel, n_dom),
        out_shape=(
            jax.ShapeDtypeStruct((Q, B, E), F32),
            jax.ShapeDtypeStruct((3, PTS, 32), F32),
        ),
        in_specs=[vmem] * 4 + [smem] + [vmem] * 10,
        out_specs=(vmem, vmem),
        scratch_shapes=[
            f32(Q, BP, E),
            f32(Q, BP, E),
            f32(Q, BP, E),
            f32(Q, 128, E),
            f32(Q, 4 * PP, E),
            b16(2 * ROWS, 4 * E),
            f32(Q, 4 * PP, E),
            f32(Q, 4 * PP, E),
            b16(4, 4 * E, E),
            b16(4, SLOTS, E),
            b16(4 * E, SLOTS),
            f32(ROWS, SLOTS),
            b16(4, 2 * ROWS, E),
            f32(128, 128),
            b16(128, 128),
            b16(128, 128),
            b16(4 * PP, 128),
            b16(48, 12 * PP),
            b16(3 * PP, 3 * PP),
            f32(13, 8, E),
            f32(4, 4, 8, E),
            f32(4, 2, 8, E),
            f32(12, 8, SLOTS),
            f32(4, PP, SLOTS),
            f32(3 * PP, SLOTS),
            f32(STEPS, 8, 48, 128),
            f32(STEPS, 8, 48, 128),
            f32(STEPS, 96, 128),
            f32(STEPS, 96, 128),
            pltpu.SemaphoreType.DMA((STEPS, 8)),
            pltpu.SemaphoreType.DMA((STEPS, 8)),
            pltpu.SemaphoreType.DMA((STEPS,)),
            pltpu.SemaphoreType.DMA((STEPS,)),
        ],
        compiler_params=pltpu.CompilerParams(
            collective_id=0, has_side_effects=True, vmem_limit_bytes=40 * 1024 * 1024
        ),
        name="ader_updates",
    )(un, gr, fn, mat, live, nc, ori, sf.reshape(1, -1), ff.reshape(1, -1), dip, coh, st, pj, lf, ro)


def solution(mesh):
    split3 = P(None, None, ("dom", "sub"))
    split2 = P(None, ("dom", "sub"))
    split1 = P(("dom", "sub"))
    placed = (
        split3, split3, split3, split2, split1, split2, split2, split1, split1, split2, split2,
        P(), P(), P(), P(),
    )
    return jax.shard_map(
        functools.partial(on_device, mesh.shape["dom"]),
        mesh=mesh,
        in_specs=placed,
        out_specs=(split3, split3),
        check_vma=False,
    )
```

profile of v0, /device:TPU:116, one launch (start us, length us, event | category | flops | bytes accessed | tf_op | source)
XLA Modules:
  0.0 26.0 jit_solution(14494516740257069610)
XLA Ops:
  0.6 0.0 copy-start.11
  1.3 0.7 %copy.17.fn = f32[4,3,256]{2,1,0:T(4,128)S(1)} copy(f32[4,3,256]{2,0,1:T(4,128)} %param.17) | data formatting | bytes 24576 | tf_op args[2]
  2.0 0.0 copy-done.11
  2.0 0.0 copy-start.12
  2.0 0.0 copy-start.6
  2.0 0.0 copy-start.7
  2.0 0.0 copy-start.10
  2.1 0.7 %copy-done.12 = f32[4,35,15]{1,0,2:T(4,128)S(1)} copy-done((f32[4,35,15]{1,0,2:T(4,128)S(1)}, f32[4,35,15]{1,0,2:T(4,128)}, u32[]{:S(2)}) %copy-start.12) | copy-done | bytes 8424
  2.8 0.0 copy-start.1
  2.8 0.0 copy-start.2
  2.8 0.0 copy-start.3
  2.8 0.0 copy-start.4
  2.8 0.0 copy-start.5
  2.8 0.0 copy-start.8
  2.8 0.0 copy-start.9
  2.8 0.1 copy.18.pj
  2.9 0.0 copy-done.6
  2.9 0.0 copy-done.7
  2.9 0.0 copy-done.10
  2.9 0.6 %copy-done.1 = f32[3,35,35]{2,1,0:T(8,128)S(1)} copy-done((f32[3,35,35]{2,1,0:T(8,128)S(1)}, f32[3,35,35]{2,1,0:T(8,128)}, u32[]{:S(2)}) %copy-start.1) | copy-done | bytes 14724
  3.6 0.0 copy-done.2
  3.6 0.0 copy-done.3
  3.6 0.0 copy-done.4
  3.6 0.0 copy-done.5
  3.6 0.0 copy-done.8
  3.6 0.0 copy-done.9
  3.6 0.0 copy-start
  3.6 1.0 %copy-done = f32[9,35,256]{2,1,0:T(8,128)S(1)} copy-done((f32[9,35,256]{2,1,0:T(8,128)S(1)}, f32[9,35,256]{2,1,0:T(8,128)}, u32[]{:S(2)}) %copy-start) | copy-done | bytes 322584
  4.6 20.0 %ader_updates.1 = (f32[9,35,256]{2,1,0:T(8,128)S(1)}, f32[3,15,32]{2,1,0:T(8,128)S(1)}) custom-call(f32[9,35,256]{2,1,0:T(8,128)S(1)} %copy-done, f32[3,3,256]{2,1,0:T(4,128)S(1)} %copy-done.3, f32[4,3,256]{2,1,0:T(4,128)S(1)} %copy.17.fn, f32[3,256]{1,0:T(4,128)S(1)} %copy-done.5, s32[1]{0:T(128)S(6)} %copy.22.live, s32[4,256]{1,0:T(4,128)S(1)} %copy-done.6, ...), custom_call_target="tpu_custom_call" | custom-call | tf_op jit(solution)/shard_map/ader_updates/pallas_call | solution.py:464
  24.6 0.7 %copy.23 = f32[9,35,256]{2,1,0:T(8,128)} copy(f32[9,35,256]{2,1,0:T(8,128)S(1)} %get-tuple-element.4) | data formatting | bytes 645120
  25.4 0.6 %copy.24 = f32[3,15,32]{2,1,0:T(8,128)} copy(f32[3,15,32]{2,1,0:T(8,128)S(1)} %get-tuple-element.5) | data formatting | bytes 11520
  (1 shorter events, 0.0 us)
Async XLA Ops:
  0.6 1.4 %copy-start.11 = (f32[4,15,35]{2,0,1:T(4,128)S(1)}, f32[4,15,35]{2,0,1:T(4,128)}, u32[]{:S(2)}) copy-start(f32[4,15,35]{2,0,1:T(4,128)} %param.28) | copy-start | bytes 25204
  2.0 0.8 %copy-start.12 = (f32[4,35,15]{1,0,2:T(4,128)S(1)}, f32[4,35,15]{1,0,2:T(4,128)}, u32[]{:S(2)}) copy-start(f32[4,35,15]{1,0,2:T(4,128)} %param.27) | copy-start | bytes 25204
  2.0 0.9 %copy-start.6 = (s32[4,256]{1,0:T(4,128)S(1)}, s32[4,256]{1,0:T(4,128)}, u32[]{:S(2)}) copy-start(s32[4,256]{1,0:T(4,128)} %nc.1) | copy-start | bytes 12292
  2.0 0.9 %copy-start.7 = (s32[4,256]{1,0:T(4,128)S(1)}, s32[4,256]{1,0:T(4,128)}, u32[]{:S(2)}) copy-start(s32[4,256]{1,0:T(4,128)} %ori.1) | copy-start | bytes 12292
  2.0 0.9 %copy-start.10 = (s32[32]{0:T(128)S(1)}, s32[32]{0:T(128)}, u32[]{:S(2)}) copy-start(s32[32]{0:T(128)} %param.23) | copy-start | bytes 388
  2.8 0.8 %copy-start.1 = (f32[3,35,35]{2,1,0:T(8,128)S(1)}, f32[3,35,35]{2,1,0:T(8,128)}, u32[]{:S(2)}) copy-start(f32[3,35,35]{2,1,0:T(8,128)} %st.1) | copy-start | bytes 44104
  2.8 0.8 %copy-start.2 = (f32[3,15,15]{2,1,0:T(8,128)S(1)}, f32[3,15,15]{2,1,0:T(8,128)}, u32[]{:S(2)}) copy-start(f32[3,15,15]{2,1,0:T(8,128)} %ro.1) | copy-start | bytes 8104
  2.8 0.8 %copy-start.3 = (f32[3,3,256]{2,1,0:T(4,128)S(1)}, f32[3,3,256]{2,1,0:T(4,128)}, u32[]{:S(2)}) copy-start(f32[3,3,256]{2,1,0:T(4,128)} %gr.1) | copy-start | bytes 27652
  2.8 0.8 %copy-start.4 = (f32[15,32]{1,0:T(8,128)S(1)}, f32[15,32]{1,0:T(8,128)}, u32[]{:S(2)}) copy-start(f32[15,32]{1,0:T(8,128)} %coh.1) | copy-start | bytes 5764
  2.8 0.8 %copy-start.5 = (f32[3,256]{1,0:T(4,128)S(1)}, f32[3,256]{1,0:T(4,128)}, u32[]{:S(2)}) copy-start(f32[3,256]{1,0:T(4,128)} %mat.1) | copy-start | bytes 9220
  2.8 0.8 %copy-start.8 = (s32[224]{0:T(256)S(1)}, s32[224]{0:T(256)}, u32[]{:S(2)}) copy-start(s32[224]{0:T(256)} %param.22) | copy-start | bytes 2692
  2.8 0.8 %copy-start.9 = (f32[2,32]{1,0:T(2,128)S(1)}, f32[2,32]{1,0:T(2,128)}, u32[]{:S(2)}) copy-start(f32[2,32]{1,0:T(2,128)} %dip.1) | copy-start | bytes 772
  3.6 1.0 %copy-start = (f32[9,35,256]{2,1,0:T(8,128)S(1)}, f32[9,35,256]{2,1,0:T(8,128)}, u32[]{:S(2)}) copy-start(f32[9,35,256]{2,1,0:T(8,128)} %un.1) | copy-start | bytes 967684
where the time goes:
time: 26.3 us; the launch traced here: 26 us
  Pallas kernels  20 us (76%)
  local copies, waits for them, and re-layouts  4.57 us (17%)
  between operations  1.4 us (5%)
    pallas_call x1, Pallas kernels, on_device(): pl.pallas_call(functools.partial(kernel, n_dom), out_shape=(jax.ShapeDtyp...  20 us
    unnamed x31, local copies, waits for them, and re-layouts  4.57 us

commit v1 on v0

v1 whole, which is shorter than its diff:
```python
import functools

import jax
import jax.numpy as jnp
from jax import lax
from jax.experimental import pallas as pl
from jax.experimental.pallas import tpu as pltpu
from jax.sharding import PartitionSpec as P

STEPS = 2
DEGREES = 4
OFFSETS = (1, 2, 3, 4, -1, -2, -3, -4)
FRICTION = 0.6
HIGHEST = lax.Precision.HIGHEST
MESH = pl.DeviceIdType.MESH

F32 = jnp.float32
BF16 = jnp.bfloat16
Q = 9
B = 35
BP = 40
PTS = 15
PP = 16
E = 256
SLOTS = 256
LANES = 128
FAULTS = 32
ROWS = Q * PP


def iota(shape, dim):
    return lax.broadcasted_iota(jnp.int32, shape, dim)


def exact_dot(a, b, dims=(((1,), (0,)), ((), ()))):
    return lax.dot_general(a, b, dims, precision=HIGHEST, preferred_element_type=F32)


def fast_dot(a, b):
    return lax.dot_general(a, b, (((1,), (0,)), ((), ())), preferred_element_type=F32)


def halves(x):
    hi = x.astype(BF16).astype(F32)
    return hi, x - hi


def elastic_rows(s, n, m):
    px, py, pz = s[6] * n[0], s[7] * n[1], s[8] * n[2]
    pressure = m[0] * (px + py + pz)
    return (
        pressure + m[1] * px,
        pressure + m[1] * py,
        pressure + m[1] * pz,
        m[2] * (s[6] * n[1] + s[7] * n[0]),
        m[2] * (s[7] * n[2] + s[8] * n[1]),
        m[2] * (s[6] * n[2] + s[8] * n[0]),
        m[3] * (s[0] * n[0] + s[3] * n[1] + s[5] * n[2]),
        m[3] * (s[3] * n[0] + s[1] * n[1] + s[4] * n[2]),
        m[3] * (s[5] * n[0] + s[4] * n[1] + s[2] * n[2]),
    )


def traction(s, n):
    return (
        s[0] * n[0] + s[3] * n[1] + s[5] * n[2],
        s[3] * n[0] + s[1] * n[1] + s[4] * n[2],
        s[5] * n[0] + s[4] * n[1] + s[2] * n[2],
    )


def kernel(
    n_dom,
    un_hbm, gr_hbm, fn_hbm, mat_hbm, nc_hbm, ori_hbm, sf_hbm, ff_hbm, dip_hbm, coh_hbm,
    st_hbm, pj_hbm, lf_hbm, ro_hbm,
    out, slip,
    un, gr, fn, mat, nc, ori, sf, ff, dip, coh, st, pj, lf, ro,
    state, cur, integ, R, tr, ths, rt, fx, p1, p2, sp, spf, hs,
    lsf, lpred, lvol, lprj, llift, lrot, coef, fcoef, turn, scoef, fcode, fdip, fric, slipsum,
    sendb, recvb, sendf, recvf,
    in_sem, send_sem, recv_sem, fsend_sem, frecv_sem,
):
    me = lax.axis_index("dom")
    sub = lax.axis_index("sub")
    partner = sub + 1 - 2 * (sub % 2)

    sources = (st_hbm, un_hbm, gr_hbm, mat_hbm, sf_hbm, pj_hbm, ff_hbm, nc_hbm, fn_hbm, ori_hbm,
               dip_hbm, coh_hbm, lf_hbm, ro_hbm)
    targets = (st, un, gr, mat, sf, pj, ff, nc, fn, ori, dip, coh, lf, ro)
    loads = [pltpu.make_async_copy(a, b, in_sem.at[j]) for j, (a, b) in enumerate(zip(sources, targets))]
    for load in loads:
        load.start()

    barrier = pltpu.get_barrier_semaphore()
    for o in OFFSETS:
        dst = me + o

        @pl.when((dst >= 0) & (dst < n_dom))
        def _():
            pl.semaphore_signal(barrier, inc=1, device_id=(dst, sub), device_id_type=MESH)

    pl.semaphore_signal(barrier, inc=1, device_id=(me, partner), device_id_type=MESH)

    for k, o in enumerate(OFFSETS):
        src = me - o

        @pl.when((src < 0) | (src >= n_dom))
        def _():
            for step in range(STEPS):
                recvb[step, 32 * k:32 * k + 32, :] = jnp.zeros((32, 128), F32)

    rep = (iota((B, 128), 0) == iota((B, 128), 1) % BP) & (iota((B, 128), 1) < 3 * BP)
    rep = jnp.where(rep, 1.0, 0.0)
    low_part = iota((128, 128), 1) >= 2 * BP
    TN = (((0,), (0,)), ((), ()))

    def stacked(x, low):
        hi, lo = halves(x)
        return jnp.where(low, lo, hi).astype(BF16)

    def spread(row):
        return jnp.broadcast_to(row, (8, E))

    place_h = jnp.where(
        ((iota((224, SLOTS), 1) & 31) < 28)
        & (iota((224, SLOTS), 0) == 28 * (iota((224, SLOTS), 1) >> 5) + (iota((224, SLOTS), 1) & 31)),
        1.0, 0.0,
    )
    unused = (iota((1, SLOTS), 1) & 31) >= 28
    lsf[...] = jnp.zeros_like(lsf)
    slipsum[...] = jnp.zeros_like(slipsum)

    loads[0].wait()
    for d in range(3):
        lsf[BP * d:BP * d + B, :] = exact_dot(st[d], rep, TN)
    lpred[...] = stacked(lsf[...], low_part)

    loads[1].wait()
    for q in range(Q):
        state[q] = jnp.concatenate([un[q], jnp.zeros((BP - B, E), F32)], axis=0)
    loads[2].wait()
    for d in range(3):
        for c in range(3):
            coef[3 * d + c] = spread(gr[d, c:c + 1, :])
    loads[3].wait()
    lam, mu, rho = mat[0:1, :], mat[1:2, :], mat[2:3, :]
    for j, row in enumerate((-lam, -2.0 * mu, -mu, -1.0 / rho)):
        coef[9 + j] = spread(row)

    loads[4].wait()
    codes = exact_dot(jnp.broadcast_to(sf[...].astype(F32), (8, 224)), place_h)
    codes = jnp.where(unused, -1, (codes[0:1, :] + 0.5).astype(jnp.int32))
    for i in range(4):
        sp[E * i:E * i + E, :] = jnp.where(iota((E, SLOTS), 0) + E * i == codes, 1.0, 0.0).astype(BF16)
    loads[5].wait()
    lsf[...] = jnp.zeros_like(lsf)
    for i in range(4):
        lsf[PP * i:PP * i + PTS, :] = exact_dot(pj[:, i, :], rep)
    lprj[...] = stacked(lsf[0:4 * PP, :], low_part[0:4 * PP])

    def setup_fault():
        loads[6].wait()
        fcode[...] = jnp.full(fcode.shape, -1, jnp.int32)
        fcode[0:1, 0:FAULTS] = ff[...]
        for i in range(4):
            hot = iota((E, LANES), 0) + E * i == fcode[0:1, :]
            spf[E * i:E * i + E, :] = jnp.where(hot, 1.0, 0.0).astype(BF16)

    def setup_rest():
        for load in loads[7:]:
            load.wait()
        for d in range(3):
            lsf[BP * d:BP * d + B, :] = exact_dot(st[d], rep)
        lvol[...] = stacked(lsf[...], low_part)
        total = jnp.zeros((B, 12 * PP), F32)
        for i in range(4):
            place = iota((PTS, 12 * PP), 1) % (4 * PP) == iota((PTS, 12 * PP), 0) + PP * i
            total = total + exact_dot(lf[:, i, :], jnp.where(place, 1.0, 0.0), TN)
        total = jnp.concatenate([total, jnp.zeros((48 - B, 12 * PP), F32)], axis=0)
        llift[...] = stacked(total, iota((48, 12 * PP), 1) >= 8 * PP)
        place = jnp.where(iota((PTS, 3 * PP), 1) % PP == iota((PTS, 3 * PP), 0), 1.0, 0.0)
        pad = jnp.zeros((PP - PTS, 3 * PP), F32)
        turns = []
        for h in range(3):
            turns += [exact_dot(ro[h], place, TN), pad]
        lrot[...] = stacked(jnp.concatenate(turns, axis=0), iota((3 * PP, 3 * PP), 1) >= 2 * PP)

        lam, mu, rho = mat[0:1, :], mat[1:2, :], mat[2:3, :]
        speed = 0.5 * jnp.sqrt((lam + 2.0 * mu) / rho)
        slip_scale = 1.0 / jnp.sqrt(mu * rho)
        slot_params = jnp.zeros((3 * PP, SLOTS + LANES), F32)
        for i in range(4):
            nx, ny, nz = fn[0, i:i + 1, :], fn[1, i:i + 1, :], fn[2, i:i + 1, :]
            cw = speed * jnp.sqrt(nx * nx + ny * ny + nz * nz)
            rows = [0.5 * nx, 0.5 * ny, 0.5 * nz, cw]
            for j, row in enumerate(rows):
                fcoef[i, j] = spread(row)
            h = ori[i:i + 1, :]
            m0 = jnp.where(h == 0, 1.0, 0.0)
            m1 = jnp.where(h == 1, 1.0, 0.0)
            turn[i, 0] = spread(m0)
            turn[i, 1] = spread(m1)
            rows += [-lam, -2.0 * mu, -mu, -1.0 / rho, slip_scale, m0, m1]
            which = iota((PP, E), 0)
            block = jnp.zeros((PP, E), F32)
            for j, row in enumerate(rows):
                block = jnp.where(which == j, jnp.broadcast_to(row, (PP, E)), block)

            code = nc[i:i + 1, :]
            for j in range(4):
                p1[i, E * j:E * j + E, :] = jnp.where(iota((E, E), 0) + E * j == code, 1.0, 0.0).astype(BF16)
            halo = code - 1024
            number = jnp.zeros_like(halo)
            for m in range(1, 8):
                number = number + jnp.where(halo >= 28 * m, 1, 0)
            fault = code - 1248
            spot = jnp.where(fault >= 0, fault + SLOTS, jnp.where(halo >= 0, halo + 4 * number, -1))
            hot = jnp.where(iota((SLOTS + LANES, E), 0) == spot, 1.0, 0.0).astype(BF16)
            p2[i] = hot
            hi, rest = halves(block)
            mid, lo = halves(rest)
            left = jnp.concatenate([hi, mid, lo], axis=0).astype(BF16)
            slot_params = slot_params + lax.dot_general(
                left, hot, (((1,), (1,)), ((), ())), preferred_element_type=F32
            )
        slot_params = slot_params[0:PP] + slot_params[PP:2 * PP] + slot_params[2 * PP:3 * PP]
        for j in range(11):
            scoef[j] = jnp.broadcast_to(slot_params[j:j + 1, :], (8, SLOTS + LANES))

        fdip[...] = jnp.zeros_like(fdip)
        fdip[0:2, 0:FAULTS] = dip[...]
        polar, azimuth = fdip[0:1, :], fdip[1:2, :]
        fric[0] = jnp.broadcast_to(jnp.sin(polar) * jnp.cos(azimuth), (PP, LANES))
        fric[1] = jnp.broadcast_to(jnp.sin(polar) * jnp.sin(azimuth), (PP, LANES))
        fric[2] = jnp.broadcast_to(jnp.cos(polar), (PP, LANES))
        fric[3] = jnp.ones((PP, LANES), F32)
        fric[3, 0:PTS, 0:FAULTS] = coh[...]

    def split_modes(x):
        hi, lo = halves(x)
        return jnp.concatenate([hi, lo, hi, jnp.zeros((8, E), F32)], axis=0).astype(BF16)

    def sum_elastic(store):
        def body(rb, carry):
            def get(q, d):
                return R[q, pl.ds(pl.multiple_of(BP * d + 8 * rb, 8), 8), :]

            g = [[coef[3 * d + c] for c in range(3)] for d in range(3)]
            m = [coef[9 + j] for j in range(4)]
            grad = {}
            for i in range(3):
                v = [get(6 + i, d) for d in range(3)]
                for c in range(3):
                    grad[i, c] = v[0] * g[0][c] + v[1] * g[1][c] + v[2] * g[2][c]
            pressure = m[0] * (grad[0, 0] + grad[1, 1] + grad[2, 2])
            res = [
                pressure + m[1] * grad[0, 0],
                pressure + m[1] * grad[1, 1],
                pressure + m[1] * grad[2, 2],
                m[2] * (grad[0, 1] + grad[1, 0]),
                m[2] * (grad[1, 2] + grad[2, 1]),
                m[2] * (grad[0, 2] + grad[2, 0]),
            ]
            for kinds in ((0, 3, 5), (3, 1, 4), (5, 4, 2)):
                force = None
                for c, q in enumerate(kinds):
                    for d in range(3):
                        term = get(q, d) * g[d][c]
                        force = term if force is None else force + term
                res.append(m[3] * force)
            store(pl.ds(pl.multiple_of(8 * rb, 8), 8), res)
            return carry

        lax.fori_loop(0, BP // 8, body, 0, unroll=True)

    def send(step, k):
        return pltpu.make_async_remote_copy(
            src_ref=sendb.at[step, pl.ds(32 * k, 32)],
            dst_ref=recvb.at[step, pl.ds(32 * k, 32)],
            send_sem=send_sem.at[step, k],
            recv_sem=recv_sem.at[step, k],
            device_id=(me + OFFSETS[k], sub),
            device_id_type=MESH,
        )

    def send_fault(step):
        return pltpu.make_async_remote_copy(
            src_ref=sendf.at[step],
            dst_ref=recvf.at[step],
            send_sem=fsend_sem.at[step],
            recv_sem=frecv_sem.at[step],
            device_id=(me, partner),
            device_id_type=MESH,
        )

    def shifted(x, by):
        return jnp.concatenate(
            [pltpu.roll(x[:, LANES * t:LANES * t + LANES], by % LANES, 1) for t in range(SLOTS // LANES)], axis=1
        )

    in_block = iota((8, SLOTS), 1) & 31
    last_row = iota((8, SLOTS), 0) == 7

    def turned(x, first, second):
        r = fast_dot(lrot[...], jnp.concatenate([x[0], x[1], x[0]], axis=0))
        return jnp.where(first, r[0:PP], jnp.where(second, r[PP:2 * PP], r[2 * PP:3 * PP]))

    def both(x):
        hi, lo = halves(x)
        return hi.astype(BF16), lo.astype(BF16)

    def slot_coefs(lanes):
        def double(j):
            return jnp.concatenate([scoef[j, :, lanes], scoef[j, :, lanes]], axis=0)

        return [double(j) for j in range(11)]

    def outer_flux(far, c):
        flux = elastic_rows(far, c[0:3], c[4:8])
        return [flux[q] - c[3] * far[q] for q in range(Q)]

    def stacked_rows(flux):
        parts = [halves(f) for f in flux]
        return jnp.concatenate([p[0] for p in parts] + [p[1] for p in parts], axis=0).astype(BF16)

    def update(step, carry):
        factor = 1.0
        for degree in range(1, DEGREES + 1):
            source = state if degree == 1 else cur
            for q in range(Q):
                R[q] = fast_dot(lpred[...], split_modes(source[q]))
            factor = factor / (degree + 1)
            base = state if degree == 1 else integ

            def store(rows, res, factor=factor, base=base):
                for q in range(Q):
                    cur[q, rows, :] = res[q]
                    integ[q, rows, :] = base[q, rows, :] + factor * res[q]

            sum_elastic(store)

        for q in range(Q):
            t = fast_dot(lprj[...], split_modes(integ[q]))
            tr[q] = t
            hi, lo = both(t)
            for i in range(4):
                ths[PP * q:PP * q + PP, E * i:E * i + E] = hi[PP * i:PP * i + PP]
                ths[ROWS + PP * q:ROWS + PP * q + PP, E * i:E * i + E] = lo[PP * i:PP * i + PP]

        picked = fast_dot(ths[...], sp[...])
        picked = picked[0:ROWS] + picked[ROWS:2 * ROWS]
        tail = picked[128 + 8:ROWS]
        tiles = []
        for t in range(16):
            x = picked[8 * t:8 * t + 8]
            if t % 2 == 1:
                x = jnp.where(last_row, jnp.broadcast_to(picked[128 + t // 2:129 + t // 2], (8, SLOTS)), x)
            if t < 7:
                x = jnp.where(in_block >= 28, shifted(tail, 28 - 4 * t), x)
            tiles.append(x)
        sendb[step] = jnp.transpose(jnp.concatenate(tiles, axis=0))

        @pl.when(step == 0)
        def _():
            pl.semaphore_wait(barrier, 1 + jnp.minimum(me, 4) + jnp.minimum(n_dom - 1 - me, 4))

        for k in (3, 7, 2, 6, 1, 5, 0, 4):
            dst = me + OFFSETS[k]

            @pl.when((dst >= 0) & (dst < n_dom))
            def _():
                send(step, k).start()

        @pl.when(step == 0)
        def _():
            setup_fault()

        picked = fast_dot(ths[...], spf[...])
        sendf[step] = picked[0:ROWS] + picked[ROWS:2 * ROWS]
        send_fault(step).start()

        @pl.when(step == 0)
        def _():
            setup_rest()

        def own_face(i, c):
            g = fast_dot(ths[...], p1[i]).astype(BF16)
            m0, m1 = turn[i, 0] > 0.5, turn[i, 1] > 0.5
            for q in range(Q):
                hi = g[PP * q:PP * q + PP]
                lo = g[ROWS + PP * q:ROWS + PP * q + PP]
                r = fast_dot(lrot[...], jnp.concatenate([hi, lo, hi], axis=0))
                for half in range(2):
                    a = 8 * half
                    rt[q, pl.ds(pl.multiple_of(PP * i + a, 8), 8), :] = jnp.where(
                        m0, r[a:a + 8], jnp.where(m1, r[PP + a:PP + a + 8], r[2 * PP + a:2 * PP + a + 8])
                    )
            m = [coef[9 + j] for j in range(4)]
            n = [fcoef[i, j] for j in range(3)]
            cw = fcoef[i, 3]
            for half in range(2):
                rows = pl.ds(pl.multiple_of(PP * i + 8 * half, 8), 8)
                own = [tr[q, rows, :] for q in range(Q)]
                far = [rt[q, rows, :] for q in range(Q)]
                res = elastic_rows([x + y for x, y in zip(own, far)], n, m)
                for q in range(Q):
                    fx[q, rows, :] = res[q] + cw * (own[q] - far[q])
            return c

        lax.fori_loop(0, 4, own_face, 0, unroll=True)

        for q in range(Q):
            R[q] = fast_dot(lvol[...], split_modes(integ[q]))

        def store_volume(rows, res):
            for q in range(Q):
                cur[q, rows, :] = state[q, rows, :] + res[q]

        sum_elastic(store_volume)

        send_fault(step).wait_recv()
        c = slot_coefs(slice(SLOTS, SLOTS + LANES))
        first, second = c[9] > 0.5, c[10] > 0.5
        far = [turned(both(recvf[step, PP * q:PP * q + PP, :]), first, second) for q in range(Q)]
        flux = outer_flux(far, c)
        u = (fric[0], fric[1], fric[2])
        mean = [0.5 * (sendf[step, PP * q:PP * q + PP, :] + far[q]) for q in range(6)]
        force = traction(mean, u)
        along = force[0] * u[0] + force[1] * u[1] + force[2] * u[2]
        tangent = [force[a] - along * u[a] for a in range(3)]
        strength = fric[3] + FRICTION * jnp.maximum(-along, 0.0)
        size = jnp.sqrt(tangent[0] * tangent[0] + tangent[1] * tangent[1] + tangent[2] * tangent[2])
        over = 1.0 - strength / jnp.maximum(size, strength)
        for a in range(3):
            excess = over * tangent[a]
            flux[6 + a] = flux[6 + a] + excess * c[7]
            slipsum[PP * a:PP * a + PP, :] += excess * c[8]
        left = stacked_rows(flux)
        for i in range(4):
            r = fast_dot(left, p2[i, SLOTS:SLOTS + LANES, :])
            for q in range(Q):
                fx[q, PP * i:PP * i + PP, :] += r[PP * q:PP * q + PP] + r[ROWS + PP * q:ROWS + PP * q + PP]

        for q in range(Q):
            hi, lo = both(fx[q])
            lifted = fast_dot(llift[...], jnp.concatenate([hi, lo, hi], axis=0))
            cur[q] = cur[q] - lifted[0:BP]

        for k, o in enumerate(OFFSETS):
            src = me - o

            @pl.when((src >= 0) & (src < n_dom))
            def _():
                send(step, k).wait_recv()

        main = jnp.transpose(recvb[step])
        tail = jnp.zeros((8, SLOTS), F32)
        for t in range(7):
            tail = jnp.where((in_block >> 2) == t, shifted(main[8 * t:8 * t + 8], 4 * t - 28), tail)
        last = jnp.concatenate([main[PP * q + PTS:PP * q + PP] for q in range(8)] + [tail], axis=0)
        c = slot_coefs(slice(0, SLOTS))
        first, second = c[9] > 0.5, c[10] > 0.5
        far = [
            turned(both(main[PP * q:PP * q + PP] if q < 8 else last), first, second) for q in range(Q)
        ]
        left = stacked_rows(outer_flux(far, c))
        for i in range(4):
            hs[i] = fast_dot(left, p2[i, 0:SLOTS, :]).astype(BF16)
        for q in range(Q):
            his = [hs[i, PP * q:PP * q + PP, :] for i in range(4)]
            los = [hs[i, ROWS + PP * q:ROWS + PP * q + PP, :] for i in range(4)]
            lifted = fast_dot(llift[...], jnp.concatenate(his + los + his, axis=0))
            state[q] = cur[q] - lifted[0:BP]
        return carry

    lax.fori_loop(0, STEPS, update, 0)

    for q in range(Q):
        out[q] = state[q, 0:B, :]
    for a in range(3):
        slip[a] = slipsum[PP * a:PP * a + PTS, 0:FAULTS]

    for step in range(STEPS):
        for k, o in enumerate(OFFSETS):
            dst = me + o

            @pl.when((dst >= 0) & (dst < n_dom))
            def _():
                send(step, k).wait_send()

        send_fault(step).wait_send()


def on_device(n_dom, *args):
    (un, gr, fn, mat, live, nc, ori, sf, ff, dip, coh, st, pj, lf, ro) = args
    fn = jnp.transpose(fn, (1, 0, 2))
    pj = jnp.transpose(pj, (2, 0, 1))
    lf = jnp.transpose(lf, (1, 0, 2))
    args = (un, gr, fn, mat, nc, ori, sf.reshape(1, -1), ff.reshape(1, -1), dip, coh, st, pj, lf, ro)
    vmem = pl.BlockSpec(memory_space=pltpu.VMEM)
    args = [pltpu.with_memory_space_constraint(a, pltpu.HBM) for a in args]

    def f32(*shape):
        return pltpu.VMEM(shape, F32)

    def b16(*shape):
        return pltpu.VMEM(shape, BF16)

    updated, slip = pl.pallas_call(
        functools.partial(kernel, n_dom),
        out_shape=(
            jax.ShapeDtypeStruct((Q, B, E), F32),
            jax.ShapeDtypeStruct((3, PTS, FAULTS), F32),
        ),
        in_specs=[pl.BlockSpec(memory_space=pltpu.HBM)] * len(args),
        out_specs=(vmem, vmem),
        scratch_shapes=[pltpu.VMEM(a.shape, a.dtype) for a in args] + [
            f32(Q, BP, E),
            f32(Q, BP, E),
            f32(Q, BP, E),
            f32(Q, 128, E),
            f32(Q, 4 * PP, E),
            b16(2 * ROWS, 4 * E),
            f32(Q, 4 * PP, E),
            f32(Q, 4 * PP, E),
            b16(4, 4 * E, E),
            b16(4, SLOTS + LANES, E),
            b16(4 * E, SLOTS),
            b16(4 * E, LANES),
            b16(4, 2 * ROWS, E),
            f32(128, 128),
            b16(128, 128),
            b16(128, 128),
            b16(4 * PP, 128),
            b16(48, 12 * PP),
            b16(3 * PP, 3 * PP),
            f32(13, 8, E),
            f32(4, 4, 8, E),
            f32(4, 2, 8, E),
            f32(11, 8, SLOTS + LANES),
            pltpu.VMEM((8, LANES), jnp.int32),
            f32(8, LANES),
            f32(4, PP, LANES),
            f32(3 * PP, LANES),
            f32(STEPS, SLOTS, LANES),
            f32(STEPS, SLOTS, LANES),
            f32(STEPS, ROWS, LANES),
            f32(STEPS, ROWS, LANES),
            pltpu.SemaphoreType.DMA((len(args),)),
            pltpu.SemaphoreType.DMA((STEPS, 8)),
            pltpu.SemaphoreType.DMA((STEPS, 8)),
            pltpu.SemaphoreType.DMA((STEPS,)),
            pltpu.SemaphoreType.DMA((STEPS,)),
        ],
        compiler_params=pltpu.CompilerParams(
            collective_id=0, has_side_effects=True, vmem_limit_bytes=40 * 1024 * 1024
        ),
        name="ader_updates",
    )(*args)
    return jnp.where(iota((1, 1, E), 2) < live[0], updated, un), slip


def solution(mesh):
    split3 = P(None, None, ("dom", "sub"))
    split2 = P(None, ("dom", "sub"))
    split1 = P(("dom", "sub"))
    placed = (
        split3, split3, split3, split2, split1, split2, split2, split1, split1, split2, split2,
        P(), P(), P(), P(),
    )
    return jax.shard_map(
        functools.partial(on_device, mesh.shape["dom"]),
        mesh=mesh,
        in_specs=placed,
        out_specs=(split3, split3),
        check_vma=False,
    )
```

time: 26.3 us -> 22.8 us (0.87)
  the two profiles are of different devices: /device:TPU:116 before, /device:TPU:103 now
where the time goes in v1:
time: 22.8 us; the launch traced here: 22.7 us
  Pallas kernels  20 us (88%)
  between operations  1.35 us (6%)
  other arithmetic  0.79 us (3%)
  local copies, waits for them, and re-layouts  0.61 us (3%)
    pallas_call x1, Pallas kernels, on_device(): pl.pallas_call(functools.partial(kernel, n_dom), out_shape=(jax.ShapeDtyp...  20 us
    select_n x1, other arithmetic, on_device(): return (jnp.where(iota((1, 1, E), 2) < live[0], updated, un), slip)  0.78 us
    unnamed x3, local copies, waits for them, and re-layouts  0.61 us

profile of v1, /device:TPU:103, one launch (start us, length us, event | category | flops | bytes accessed | tf_op | source)
XLA Modules:
  0.0 22.7 jit_solution(4106190279967002459)
XLA Ops:
  0.6 0.0 copy-start
  1.3 20.0 %ader_updates.1 = (f32[9,35,256]{2,1,0:T(8,128)S(1)}, f32[3,15,32]{2,1,0:T(8,128)S(1)}) custom-call(f32[9,35,256]{2,1,0:T(8,128)} %un_hbm.1, f32[3,3,256]{2,1,0:T(4,128)} %gr_hbm.1, f32[3,4,256]{2,1,0:T(4,128)} %bitcast.9, f32[3,256]{1,0:T(4,128)} %mat_hbm.1, s32[4,256]{1,0:T(4,128)} %nc_hbm.1, s32[4,256]{1,0:T(4,128)} %ori_hbm.1, s32[1,224]{1,0:T(1,128)} %bitcast.10, ...), custom_call_target="tpu_custom_call" | custom-call | tf_op jit(solution)/shard_map/ader_updates/pallas_call | solution.py:509
  21.3 0.0 copy-done
  21.3 0.8 %broadcast_select_fusion = f32[9,35,256]{2,1,0:T(8,128)} fusion(f32[9,35,256]{2,1,0:T(8,128)S(1)} %get-tuple-element.4, f32[9,35,256]{2,1,0:T(8,128)S(1)} %copy-done, pred[256]{0:T(512)(128)(4,1)S(1)} %iota_compare_fusion), kind=kLoop, calls=%fused_computation | loop fusion | flops 80640 | bytes 967936 | tf_op jit(solution)/shard_map/jit(_where)/select_n | solution.py:560
  22.1 0.6 %copy.19 = f32[3,15,32]{2,1,0:T(8,128)} copy(f32[3,15,32]{2,1,0:T(8,128)S(1)} %get-tuple-element.9) | data formatting | bytes 11520
  (1 shorter events, 0.0 us)
Async XLA Ops:
  0.6 20.7 %copy-start = (f32[9,35,256]{2,1,0:T(8,128)S(1)}, f32[9,35,256]{2,1,0:T(8,128)}, u32[]{:S(2)}) copy-start(f32[9,35,256]{2,1,0:T(8,128)} %un_hbm.1) | copy-start | bytes 967684

commit v2 on v1

--- a/solution.py
+++ b/solution.py
@@ -36,8 +36,8 @@
     return lax.dot_general(a, b, dims, precision=HIGHEST, preferred_element_type=F32)
 
 
-def fast_dot(a, b):
-    return lax.dot_general(a, b, (((1,), (0,)), ((), ())), preferred_element_type=F32)
+def fast_dot(a, b, dims=(((1,), (0,)), ((), ()))):
+    return lax.dot_general(a, b, dims, preferred_element_type=F32)
 
 
 def halves(x):
@@ -76,7 +76,7 @@
     out, slip,
     un, gr, fn, mat, nc, ori, sf, ff, dip, coh, st, pj, lf, ro,
     state, cur, integ, R, tr, ths, rt, fx, p1, p2, sp, spf, hs,
-    lsf, lpred, lvol, lprj, llift, lrot, coef, fcoef, turn, scoef, fcode, fdip, fric, slipsum,
+    lsf, lsp, lpred, lvol, lprj, llift, lrot, coef, fcoef, turn, scoef, fcode, fdip, fric, slipsum,
     sendb, recvb, sendf, recvf,
     in_sem, send_sem, recv_sem, fsend_sem, frecv_sem,
 ):
@@ -110,13 +110,25 @@
                 recvb[step, 32 * k:32 * k + 32, :] = jnp.zeros((32, 128), F32)
 
     rep = (iota((B, 128), 0) == iota((B, 128), 1) % BP) & (iota((B, 128), 1) < 3 * BP)
-    rep = jnp.where(rep, 1.0, 0.0)
-    low_part = iota((128, 128), 1) >= 2 * BP
+    low_part = iota((B, 128), 1) >= 2 * BP
+    rep_hi = jnp.where(rep & ~low_part, 1.0, 0.0).astype(BF16)
+    rep_lo = jnp.where(rep & low_part, 1.0, 0.0).astype(BF16)
+    row, col = iota((2 * BP, 128), 0), iota((2 * BP, 128), 1)
+    rep2 = (row % BP == col % BP) & (row % BP < B) & (col < 3 * BP) & ((row >= BP) == (col >= 2 * BP))
+    rep2 = jnp.where(rep2, 1.0, 0.0).astype(BF16)
     TN = (((0,), (0,)), ((), ()))
 
     def stacked(x, low):
         hi, lo = halves(x)
         return jnp.where(low, lo, hi).astype(BF16)
+
+    def both(x):
+        hi, lo = halves(x)
+        return hi.astype(BF16), lo.astype(BF16)
+
+    def stack_low(x):
+        hi, lo = halves(jnp.concatenate([x, jnp.zeros((BP - B, x.shape[1]), F32)], axis=0))
+        return jnp.concatenate([hi, lo], axis=0).astype(BF16)
 
     def spread(row):
         return jnp.broadcast_to(row, (8, E))
@@ -130,33 +142,33 @@
     lsf[...] = jnp.zeros_like(lsf)
     slipsum[...] = jnp.zeros_like(slipsum)
 
-    loads[0].wait()
+    for load in loads[0:6]:
+        load.wait()
     for d in range(3):
-        lsf[BP * d:BP * d + B, :] = exact_dot(st[d], rep, TN)
-    lpred[...] = stacked(lsf[...], low_part)
-
-    loads[1].wait()
+        lsf[BP * d:BP * d + B, :] = fast_dot(stack_low(st[d]), rep2, TN)
+    lpred[...] = lsf[...].astype(BF16)
+
     for q in range(Q):
         state[q] = jnp.concatenate([un[q], jnp.zeros((BP - B, E), F32)], axis=0)
-    loads[2].wait()
     for d in range(3):
         for c in range(3):
             coef[3 * d + c] = spread(gr[d, c:c + 1, :])
-    loads[3].wait()
     lam, mu, rho = mat[0:1, :], mat[1:2, :], mat[2:3, :]
     for j, row in enumerate((-lam, -2.0 * mu, -mu, -1.0 / rho)):
         coef[9 + j] = spread(row)
 
-    loads[4].wait()
-    codes = exact_dot(jnp.broadcast_to(sf[...].astype(F32), (8, 224)), place_h)
-    codes = jnp.where(unused, -1, (codes[0:1, :] + 0.5).astype(jnp.int32))
+    raw = jnp.broadcast_to(sf[...], (8, 224))
+    raw = jnp.concatenate([raw >> 8, raw & 255], axis=0).astype(F32).astype(BF16)
+    placed = fast_dot(raw, place_h.astype(BF16))
+    codes = (placed[0:1, :] * 256.0 + placed[8:9, :] + 0.5).astype(jnp.int32)
+    codes = jnp.where(unused, -1, codes)
     for i in range(4):
         sp[E * i:E * i + E, :] = jnp.where(iota((E, SLOTS), 0) + E * i == codes, 1.0, 0.0).astype(BF16)
-    loads[5].wait()
-    lsf[...] = jnp.zeros_like(lsf)
+    lsp[...] = jnp.zeros_like(lsp)
     for i in range(4):
-        lsf[PP * i:PP * i + PTS, :] = exact_dot(pj[:, i, :], rep)
-    lprj[...] = stacked(lsf[0:4 * PP, :], low_part[0:4 * PP])
+        hi, lo = both(pj[:, i, :])
+        lsp[PP * i:PP * i + PTS, :] = fast_dot(hi, rep_hi) + fast_dot(lo, rep_lo)
+    lprj[...] = lsp[...].astype(BF16)
 
     def setup_fault():
         loads[6].wait()
@@ -170,8 +182,9 @@
         for load in loads[7:]:
             load.wait()
         for d in range(3):
-            lsf[BP * d:BP * d + B, :] = exact_dot(st[d], rep)
-        lvol[...] = stacked(lsf[...], low_part)
+            hi, lo = both(st[d])
+            lsf[BP * d:BP * d + B, :] = fast_dot(hi, rep_hi) + fast_dot(lo, rep_lo)
+        lvol[...] = lsf[...].astype(BF16)
         total = jnp.zeros((B, 12 * PP), F32)
         for i in range(4):
             place = iota((PTS, 12 * PP), 1) % (4 * PP) == iota((PTS, 12 * PP), 0) + PP * i
@@ -305,10 +318,6 @@
         r = fast_dot(lrot[...], jnp.concatenate([x[0], x[1], x[0]], axis=0))
         return jnp.where(first, r[0:PP], jnp.where(second, r[PP:2 * PP], r[2 * PP:3 * PP]))
 
-    def both(x):
-        hi, lo = halves(x)
-        return hi.astype(BF16), lo.astype(BF16)
-
     def slot_coefs(lanes):
         def double(j):
             return jnp.concatenate([scoef[j, :, lanes], scoef[j, :, lanes]], axis=0)
@@ -323,7 +332,7 @@
         parts = [halves(f) for f in flux]
         return jnp.concatenate([p[0] for p in parts] + [p[1] for p in parts], axis=0).astype(BF16)
 
-    def update(step, carry):
+    def update(step):
         factor = 1.0
         for degree in range(1, DEGREES + 1):
             source = state if degree == 1 else cur
@@ -360,8 +369,7 @@
             tiles.append(x)
         sendb[step] = jnp.transpose(jnp.concatenate(tiles, axis=0))
 
-        @pl.when(step == 0)
-        def _():
+        if step == 0:
             pl.semaphore_wait(barrier, 1 + jnp.minimum(me, 4) + jnp.minimum(n_dom - 1 - me, 4))
 
         for k in (3, 7, 2, 6, 1, 5, 0, 4):
@@ -371,16 +379,14 @@
             def _():
                 send(step, k).start()
 
-        @pl.when(step == 0)
-        def _():
+        if step == 0:
             setup_fault()
 
         picked = fast_dot(ths[...], spf[...])
         sendf[step] = picked[0:ROWS] + picked[ROWS:2 * ROWS]
         send_fault(step).start()
 
-        @pl.when(step == 0)
-        def _():
+        if step == 0:
             setup_rest()
 
         def own_face(i, c):
@@ -471,9 +477,9 @@
             los = [hs[i, ROWS + PP * q:ROWS + PP * q + PP, :] for i in range(4)]
             lifted = fast_dot(llift[...], jnp.concatenate(his + los + his, axis=0))
             state[q] = cur[q] - lifted[0:BP]
-        return carry
-
-    lax.fori_loop(0, STEPS, update, 0)
+
+    for step in range(STEPS):
+        update(step)
 
     for q in range(Q):
         out[q] = state[q, 0:B, :]
@@ -529,6 +535,7 @@
             b16(4 * E, LANES),
             b16(4, 2 * ROWS, E),
             f32(128, 128),
+            f32(4 * PP, 128),
             b16(128, 128),
             b16(128, 128),
             b16(4 * PP, 128),

time: 22.8 us -> 22.1 us (0.969)
  Pallas kernels: 20 us -> 19.2 us
    pallas_call x1, Pallas kernels: 20 us -> 19.2 us  [on_device(): pl.pallas_call(functools.partial(kernel, n_dom), out_shape=(jax.ShapeDtyp...]
where the time goes in v2:
time: 22.1 us; the launch traced here: 22 us
  Pallas kernels  19.2 us (87%)
  between operations  1.35 us (6%)
  other arithmetic  0.79 us (4%)
  local copies, waits for them, and re-layouts  0.61 us (3%)
    pallas_call x1, Pallas kernels, on_device(): pl.pallas_call(functools.partial(kernel, n_dom), out_shape=(jax.ShapeDtyp...  19.2 us
    select_n x1, other arithmetic, on_device(): return (jnp.where(iota((1, 1, E), 2) < live[0], updated, un), slip)  0.78 us
    unnamed x3, local copies, waits for them, and re-layouts  0.61 us

profile of v2, /device:TPU:103, one launch (start us, length us, event | category | flops | bytes accessed | tf_op | source)
XLA Modules:
  0.0 22.0 jit_solution(17453527312771662063)
XLA Ops:
  0.6 0.0 copy-start
  1.3 19.2 %ader_updates.1 = (f32[9,35,256]{2,1,0:T(8,128)S(1)}, f32[3,15,32]{2,1,0:T(8,128)S(1)}) custom-call(f32[9,35,256]{2,1,0:T(8,128)} %un_hbm.1, f32[3,3,256]{2,1,0:T(4,128)} %gr_hbm.1, f32[3,4,256]{2,1,0:T(4,128)} %bitcast.9, f32[3,256]{1,0:T(4,128)} %mat_hbm.1, s32[4,256]{1,0:T(4,128)} %nc_hbm.1, s32[4,256]{1,0:T(4,128)} %ori_hbm.1, s32[1,224]{1,0:T(1,128)} %bitcast.10, ...), custom_call_target="tpu_custom_call" | custom-call | tf_op jit(solution)/shard_map/ader_updates/pallas_call | solution.py:515
  20.6 0.0 copy-done
  20.6 0.8 %broadcast_select_fusion = f32[9,35,256]{2,1,0:T(8,128)} fusion(f32[9,35,256]{2,1,0:T(8,128)S(1)} %get-tuple-element.4, f32[9,35,256]{2,1,0:T(8,128)S(1)} %copy-done, pred[256]{0:T(512)(128)(4,1)S(1)} %iota_compare_fusion), kind=kLoop, calls=%fused_computation | loop fusion | flops 80640 | bytes 967936 | tf_op jit(solution)/shard_map/jit(_where)/select_n | solution.py:567
  21.4 0.6 %copy.19 = f32[3,15,32]{2,1,0:T(8,128)} copy(f32[3,15,32]{2,1,0:T(8,128)S(1)} %get-tuple-element.9) | data formatting | bytes 11520
  (1 shorter events, 0.0 us)
Async XLA Ops:
  0.6 20.0 %copy-start = (f32[9,35,256]{2,1,0:T(8,128)S(1)}, f32[9,35,256]{2,1,0:T(8,128)}, u32[]{:S(2)}) copy-start(f32[9,35,256]{2,1,0:T(8,128)} %un_hbm.1) | copy-start | bytes 967684

commit v3 on v2

--- a/solution.py
+++ b/solution.py
@@ -25,6 +25,7 @@
 SLOTS = 256
 LANES = 128
 FAULTS = 32
+PARTS = 3
 ROWS = Q * PP
 
 
@@ -76,8 +77,8 @@
     out, slip,
     un, gr, fn, mat, nc, ori, sf, ff, dip, coh, st, pj, lf, ro,
     state, cur, integ, R, tr, ths, rt, fx, p1, p2, sp, spf, hs,
-    lsf, lsp, lpred, lvol, lprj, llift, lrot, coef, fcoef, turn, scoef, fcode, fdip, fric, slipsum,
-    sendb, recvb, sendf, recvf,
+    pull, drive, lsf, lsp, lforce, lpred, lvol, lprj, llift, lrot, coef, fcoef, turn, scoef, fcode, fdip, fric, slipsum,
+    sendb, recvb, sgf, sendf, recvf,
     in_sem, send_sem, recv_sem, fsend_sem, frecv_sem,
 ):
     me = lax.axis_index("dom")
@@ -147,6 +148,14 @@
     for d in range(3):
         lsf[BP * d:BP * d + B, :] = fast_dot(stack_low(st[d]), rep2, TN)
     lpred[...] = lsf[...].astype(BF16)
+    row, col = iota((2 * BP, 384), 0), iota((2 * BP, 384), 1)
+    total = jnp.zeros((B, 384), F32)
+    for d in range(3):
+        inner = col - 3 * BP * d
+        hot = (row % BP == col % BP) & (row % BP < B) & (inner >= 0) & (inner < 3 * BP)
+        hot = jnp.where(hot & ((row >= BP) == (inner >= 2 * BP)), 1.0, 0.0).astype(BF16)
+        total = total + fast_dot(stack_low(st[d]), hot, TN)
+    lforce[...] = jnp.concatenate([total, jnp.zeros((48 - B, 384), F32)], axis=0).astype(BF16)
 
     for q in range(Q):
         state[q] = jnp.concatenate([un[q], jnp.zeros((BP - B, E), F32)], axis=0)
@@ -333,20 +342,63 @@
         return jnp.concatenate([p[0] for p in parts] + [p[1] for p in parts], axis=0).astype(BF16)
 
     def update(step):
+        def forces(rows, sigma):
+            g = [[coef[3 * d + c] for c in range(3)] for d in range(3)]
+            for c, kinds in enumerate(((0, 3, 5), (3, 1, 4), (5, 4, 2))):
+                for d in range(3):
+                    pull[3 * c + d, rows, :] = (
+                        sigma[kinds[0]] * g[d][0] + sigma[kinds[1]] * g[d][1] + sigma[kinds[2]] * g[d][2]
+                    )
+
+        def first(rb, carry):
+            rows = pl.ds(pl.multiple_of(8 * rb, 8), 8)
+            forces(rows, [state[q, rows, :] for q in range(6)])
+            return carry
+
+        lax.fori_loop(0, BP // 8, first, 0, unroll=True)
         factor = 1.0
         for degree in range(1, DEGREES + 1):
-            source = state if degree == 1 else cur
-            for q in range(Q):
-                R[q] = fast_dot(lpred[...], split_modes(source[q]))
+            for i in range(3):
+                x = state[6 + i] if degree == 1 else cur[6 + i]
+                R[i] = fast_dot(lpred[...], split_modes(x))
+            for c in range(3):
+                pieces = []
+                for d in range(3):
+                    hi, lo = halves(pull[3 * c + d])
+                    pieces += [hi, lo, hi]
+                pieces = jnp.concatenate(pieces + [jnp.zeros((24, E), F32)], axis=0).astype(BF16)
+                drive[c] = fast_dot(lforce[...], pieces)
             factor = factor / (degree + 1)
-            base = state if degree == 1 else integ
-
-            def store(rows, res, factor=factor, base=base):
+
+            def body(rb, carry, factor=factor, degree=degree):
+                rows = pl.ds(pl.multiple_of(8 * rb, 8), 8)
+                g = [[coef[3 * d + c] for c in range(3)] for d in range(3)]
+                m = [coef[9 + j] for j in range(4)]
+                grad = {}
+                for i in range(3):
+                    v = [R[i, pl.ds(pl.multiple_of(BP * d + 8 * rb, 8), 8), :] for d in range(3)]
+                    for c in range(3):
+                        grad[i, c] = v[0] * g[0][c] + v[1] * g[1][c] + v[2] * g[2][c]
+                pressure = m[0] * (grad[0, 0] + grad[1, 1] + grad[2, 2])
+                res = [
+                    pressure + m[1] * grad[0, 0],
+                    pressure + m[1] * grad[1, 1],
+                    pressure + m[1] * grad[2, 2],
+                    m[2] * (grad[0, 1] + grad[1, 0]),
+                    m[2] * (grad[1, 2] + grad[2, 1]),
+                    m[2] * (grad[0, 2] + grad[2, 0]),
+                ]
+                res += [m[3] * drive[c, rows, :] for c in range(3)]
+                base = state if degree == 1 else integ
                 for q in range(Q):
-                    cur[q, rows, :] = res[q]
                     integ[q, rows, :] = base[q, rows, :] + factor * res[q]
-
-            sum_elastic(store)
+                if degree < DEGREES:
+                    for i in range(3):
+                        cur[6 + i, rows, :] = res[6 + i]
+                    forces(rows, res[0:6])
+                return carry
+
+            lax.fori_loop(0, BP // 8, body, 0, unroll=True)
 
         for q in range(Q):
             t = fast_dot(lprj[...], split_modes(integ[q]))
@@ -383,7 +435,13 @@
             setup_fault()
 
         picked = fast_dot(ths[...], spf[...])
-        sendf[step] = picked[0:ROWS] + picked[ROWS:2 * ROWS]
+        picked = picked[0:ROWS] + picked[ROWS:2 * ROWS]
+        sgf[...] = picked
+        sendf[step] = (
+            picked[0:3 * PP]
+            + pltpu.roll(picked[3 * PP:6 * PP], FAULTS, 1)
+            + pltpu.roll(picked[6 * PP:9 * PP], 2 * FAULTS, 1)
+        )
         send_fault(step).start()
 
         if step == 0:
@@ -427,10 +485,13 @@
         send_fault(step).wait_recv()
         c = slot_coefs(slice(SLOTS, SLOTS + LANES))
         first, second = c[9] > 0.5, c[10] > 0.5
-        far = [turned(both(recvf[step, PP * q:PP * q + PP, :]), first, second) for q in range(Q)]
+        came = recvf[step]
+        came = [came, pltpu.roll(came, LANES - FAULTS, 1), pltpu.roll(came, LANES - 2 * FAULTS, 1)]
+        came = jnp.concatenate(came, axis=0)
+        far = [turned(both(came[PP * q:PP * q + PP]), first, second) for q in range(Q)]
         flux = outer_flux(far, c)
         u = (fric[0], fric[1], fric[2])
-        mean = [0.5 * (sendf[step, PP * q:PP * q + PP, :] + far[q]) for q in range(6)]
+        mean = [0.5 * (sgf[PP * q:PP * q + PP, :] + far[q]) for q in range(6)]
         force = traction(mean, u)
         along = force[0] * u[0] + force[1] * u[1] + force[2] * u[2]
         tangent = [force[a] - along * u[a] for a in range(3)]
@@ -495,6 +556,21 @@
                 send(step, k).wait_send()
 
         send_fault(step).wait_send()
+
+
+def select_live(live, un, updated, slip, out_hbm, slip_hbm, out, sem):
+    copies = [pltpu.make_async_copy(slip, slip_hbm, sem.at[PARTS])]
+    copies[0].start()
+    alive = jnp.broadcast_to(iota((1, E), 1) < live[0:1, 0:1], (B, E))
+    size = Q // PARTS
+    for part in range(PARTS):
+        for q in range(part * size, part * size + size):
+            out[q] = jnp.where(alive, updated[q], un[q])
+        rows = pl.ds(part * size, size)
+        copies.append(pltpu.make_async_copy(out.at[rows], out_hbm.at[rows], sem.at[part]))
+        copies[-1].start()
+    for copy in copies:
+        copy.wait()
 
 
 def on_device(n_dom, *args):
@@ -534,8 +610,11 @@
             b16(4 * E, SLOTS),
             b16(4 * E, LANES),
             b16(4, 2 * ROWS, E),
+            f32(Q, BP, E),
+            f32(3, 48, E),
             f32(128, 128),
             f32(4 * PP, 128),
+            b16(48, 384),
             b16(128, 128),
             b16(128, 128),
             b16(4 * PP, 128),
@@ -551,8 +630,9 @@
             f32(3 * PP, LANES),
             f32(STEPS, SLOTS, LANES),
             f32(STEPS, SLOTS, LANES),
-            f32(STEPS, ROWS, LANES),
-            f32(STEPS, ROWS, LANES),
+            f32(ROWS, LANES),
+            f32(STEPS, 3 * PP, LANES),
+            f32(STEPS, 3 * PP, LANES),
             pltpu.SemaphoreType.DMA((len(args),)),
             pltpu.SemaphoreType.DMA((STEPS, 8)),
             pltpu.SemaphoreType.DMA((STEPS, 8)),
@@ -564,7 +644,20 @@
         ),
         name="ader_updates",
     )(*args)
-    return jnp.where(iota((1, 1, E), 2) < live[0], updated, un), slip
+    live = lax.pad(live, jnp.int32(0), ((0, LANES - 1, 0),)).reshape(1, LANES)
+    hbm = pl.BlockSpec(memory_space=pl.ANY)
+    return pl.pallas_call(
+        select_live,
+        out_shape=(
+            jax.ShapeDtypeStruct((Q, B, E), F32),
+            jax.ShapeDtypeStruct((3, PTS, FAULTS), F32),
+        ),
+        in_specs=[vmem] * 4,
+        out_specs=(hbm, hbm),
+        scratch_shapes=[f32(Q, B, E), pltpu.SemaphoreType.DMA((PARTS + 1,))],
+        compiler_params=pltpu.CompilerParams(vmem_limit_bytes=4 * 1024 * 1024),
+        name="select_live",
+    )(live, un, updated, slip)
 
 
 def solution(mesh):

time: 22.1 us -> 20.6 us (0.932)
  other arithmetic: 0.79 us -> 0 us
  local copies, waits for them, and re-layouts: 0.61 us -> 0.01 us
    pallas_call x1, Pallas kernels: 19.2 us -> 18.3 us  [on_device(): pl.pallas_call(functools.partial(kernel, n_dom), out_shape=(jax.ShapeDtyp...]
    pallas_call x0 -> x1, Pallas kernels: none -> 0.85 us  [on_device(): pl.pallas_call(select_live, out_shape=(jax.ShapeDtypeStruct((Q, B, E), F3...]
    select_n x1 -> x0, other arithmetic: 0.78 us -> none  [on_device(): return (jnp.where(iota((1, 1, E), 2) < live[0], updated, un), slip)]
    unnamed x3 -> x2, local copies, waits for them, and re-layouts: 0.61 us -> 0.01 us
where the time goes in v3:
time: 20.6 us; the launch traced here: 20.5 us
  Pallas kernels  19.1 us (93%)
  between operations  1.36 us (7%)
    pallas_call x1, Pallas kernels, on_device(): pl.pallas_call(functools.partial(kernel, n_dom), out_shape=(jax.ShapeDtyp...  18.3 us
    pallas_call x1, Pallas kernels, on_device(): pl.pallas_call(select_live, out_shape=(jax.ShapeDtypeStruct((Q, B, E), F3...  0.85 us

profile of v3, /device:TPU:103, one launch (start us, length us, event | category | flops | bytes accessed | tf_op | source)
XLA Modules:
  0.0 20.5 jit_solution(15281960243182481506)
XLA Ops:
  0.6 0.0 copy-start
  1.3 18.3 %ader_updates.1 = (f32[9,35,256]{2,1,0:T(8,128)S(1)}, f32[3,15,32]{2,1,0:T(8,128)S(1)}) custom-call(f32[9,35,256]{2,1,0:T(8,128)} %un.1, f32[3,3,256]{2,1,0:T(4,128)} %gr_hbm.1, f32[3,4,256]{2,1,0:T(4,128)} %bitcast.9, f32[3,256]{1,0:T(4,128)} %mat_hbm.1, s32[4,256]{1,0:T(4,128)} %nc_hbm.1, s32[4,256]{1,0:T(4,128)} %ori_hbm.1, s32[1,224]{1,0:T(1,128)} %bitcast.10, ...), custom_call_target="tpu_custom_call" | custom-call | tf_op jit(solution)/shard_map/ader_updates/pallas_call | solution.py:591
  19.6 0.0 copy-done
  19.6 0.8 %select_live.1 = (f32[9,35,256]{2,1,0:T(8,128)}, f32[3,15,32]{2,1,0:T(8,128)}) custom-call(s32[1,128]{1,0:T(1,128)S(1)} %pad_bitcast_fusion.live, f32[9,35,256]{2,1,0:T(8,128)S(1)} %copy-done, f32[9,35,256]{2,1,0:T(8,128)S(1)} %get-tuple-element.4.updated, f32[3,15,32]{2,1,0:T(8,128)S(1)} %get-tuple-element.5.slip), custom_call_target="tpu_custom_call" | custom-call | tf_op jit(solution)/shard_map/select_live/pallas_call | solution.py:649
  (1 shorter events, 0.0 us)
Async XLA Ops:
  0.6 19.0 %copy-start = (f32[9,35,256]{2,1,0:T(8,128)S(1)}, f32[9,35,256]{2,1,0:T(8,128)}, u32[]{:S(2)}) copy-start(f32[9,35,256]{2,1,0:T(8,128)} %un.1) | copy-start | bytes 967684

commit v4 on v3

--- a/solution.py
+++ b/solution.py
@@ -514,7 +514,16 @@
             cur[q] = cur[q] - lifted[0:BP]
 
         for k, o in enumerate(OFFSETS):
-            src = me - o
+            dst = me + o
+
+            @pl.when((dst >= 0) & (dst < n_dom))
+            def _():
+                send(step, k).wait_send()
+
+        send_fault(step).wait_send()
+
+        for k in (0, 4, 1, 5, 2, 6, 3, 7):
+            src = me - OFFSETS[k]
 
             @pl.when((src >= 0) & (src < n_dom))
             def _():
@@ -537,25 +546,16 @@
             his = [hs[i, PP * q:PP * q + PP, :] for i in range(4)]
             los = [hs[i, ROWS + PP * q:ROWS + PP * q + PP, :] for i in range(4)]
             lifted = fast_dot(llift[...], jnp.concatenate(his + los + his, axis=0))
-            state[q] = cur[q] - lifted[0:BP]
+            if step < STEPS - 1:
+                state[q] = cur[q] - lifted[0:BP]
+            else:
+                out[q] = cur[q, 0:B, :] - lifted[0:B]
 
     for step in range(STEPS):
         update(step)
 
-    for q in range(Q):
-        out[q] = state[q, 0:B, :]
     for a in range(3):
         slip[a] = slipsum[PP * a:PP * a + PTS, 0:FAULTS]
-
-    for step in range(STEPS):
-        for k, o in enumerate(OFFSETS):
-            dst = me + o
-
-            @pl.when((dst >= 0) & (dst < n_dom))
-            def _():
-                send(step, k).wait_send()
-
-        send_fault(step).wait_send()
 
 
 def select_live(live, un, updated, slip, out_hbm, slip_hbm, out, sem):

time: 20.6 us -> 20.6 us (level)
  no operation moved by 1% of the time
where the time goes in v4:
time: 20.6 us; the launch traced here: 20.4 us
  Pallas kernels  19.1 us (93%)
  between operations  1.36 us (7%)
    pallas_call x1, Pallas kernels, on_device(): pl.pallas_call(functools.partial(kernel, n_dom), out_shape=(jax.ShapeDtyp...  18.2 us
    pallas_call x1, Pallas kernels, on_device(): pl.pallas_call(select_live, out_shape=(jax.ShapeDtypeStruct((Q, B, E), F3...  0.85 us

profile of v4, /device:TPU:103, one launch (start us, length us, event | category | flops | bytes accessed | tf_op | source)
XLA Modules:
  0.0 20.4 jit_solution(17043577855826082052)
XLA Ops:
  0.6 0.0 copy-start
  1.3 18.2 %ader_updates.1 = (f32[9,35,256]{2,1,0:T(8,128)S(1)}, f32[3,15,32]{2,1,0:T(8,128)S(1)}) custom-call(f32[9,35,256]{2,1,0:T(8,128)} %un.1, f32[3,3,256]{2,1,0:T(4,128)} %gr_hbm.1, f32[3,4,256]{2,1,0:T(4,128)} %bitcast.9, f32[3,256]{1,0:T(4,128)} %mat_hbm.1, s32[4,256]{1,0:T(4,128)} %nc_hbm.1, s32[4,256]{1,0:T(4,128)} %ori_hbm.1, s32[1,224]{1,0:T(1,128)} %bitcast.10, ...), custom_call_target="tpu_custom_call" | custom-call | tf_op jit(solution)/shard_map/ader_updates/pallas_call | solution.py:591
  19.6 0.0 copy-done
  19.6 0.8 %select_live.1 = (f32[9,35,256]{2,1,0:T(8,128)}, f32[3,15,32]{2,1,0:T(8,128)}) custom-call(s32[1,128]{1,0:T(1,128)S(1)} %pad_bitcast_fusion.live, f32[9,35,256]{2,1,0:T(8,128)S(1)} %copy-done, f32[9,35,256]{2,1,0:T(8,128)S(1)} %get-tuple-element.4.updated, f32[3,15,32]{2,1,0:T(8,128)S(1)} %get-tuple-element.5.slip), custom_call_target="tpu_custom_call" | custom-call | tf_op jit(solution)/shard_map/select_live/pallas_call | solution.py:649
  (1 shorter events, 0.0 us)
Async XLA Ops:
  0.6 19.0 %copy-start = (f32[9,35,256]{2,1,0:T(8,128)S(1)}, f32[9,35,256]{2,1,0:T(8,128)}, u32[]{:S(2)}) copy-start(f32[9,35,256]{2,1,0:T(8,128)} %un.1) | copy-start | bytes 967684

commit v5 on v4

--- a/solution.py
+++ b/solution.py
@@ -84,6 +84,7 @@
     me = lax.axis_index("dom")
     sub = lax.axis_index("sub")
     partner = sub + 1 - 2 * (sub % 2)
+    inside = (me >= 4) & (me < n_dom - 4)
 
     sources = (st_hbm, un_hbm, gr_hbm, mat_hbm, sf_hbm, pj_hbm, ff_hbm, nc_hbm, fn_hbm, ori_hbm,
                dip_hbm, coh_hbm, lf_hbm, ro_hbm)
@@ -424,12 +425,21 @@
         if step == 0:
             pl.semaphore_wait(barrier, 1 + jnp.minimum(me, 4) + jnp.minimum(n_dom - 1 - me, 4))
 
-        for k in (3, 7, 2, 6, 1, 5, 0, 4):
-            dst = me + OFFSETS[k]
-
-            @pl.when((dst >= 0) & (dst < n_dom))
-            def _():
+        far_first = (3, 7, 2, 6, 1, 5, 0, 4)
+
+        @pl.when(inside)
+        def _():
+            for k in far_first:
                 send(step, k).start()
+
+        @pl.when(jnp.logical_not(inside))
+        def _():
+            for k in far_first:
+                dst = me + OFFSETS[k]
+
+                @pl.when((dst >= 0) & (dst < n_dom))
+                def _():
+                    send(step, k).start()
 
         if step == 0:
             setup_fault()

time: 20.6 us -> 20.6 us (level)
  no operation moved by 1% of the time
where the time goes in v5:
time: 20.6 us; the launch traced here: 20.5 us
  Pallas kernels  19.1 us (93%)
  between operations  1.36 us (7%)
    pallas_call x1, Pallas kernels, on_device(): pl.pallas_call(functools.partial(kernel, n_dom), out_shape=(jax.ShapeDtyp...  18.3 us
    pallas_call x1, Pallas kernels, on_device(): pl.pallas_call(select_live, out_shape=(jax.ShapeDtypeStruct((Q, B, E), F3...  0.85 us

profile of v5, /device:TPU:103, one launch (start us, length us, event | category | flops | bytes accessed | tf_op | source)
XLA Modules:
  0.0 20.5 jit_solution(8035650814484909018)
XLA Ops:
  0.6 0.0 copy-start
  1.3 18.3 %ader_updates.1 = (f32[9,35,256]{2,1,0:T(8,128)S(1)}, f32[3,15,32]{2,1,0:T(8,128)S(1)}) custom-call(f32[9,35,256]{2,1,0:T(8,128)} %un.1, f32[3,3,256]{2,1,0:T(4,128)} %gr_hbm.1, f32[3,4,256]{2,1,0:T(4,128)} %bitcast.9, f32[3,256]{1,0:T(4,128)} %mat_hbm.1, s32[4,256]{1,0:T(4,128)} %nc_hbm.1, s32[4,256]{1,0:T(4,128)} %ori_hbm.1, s32[1,224]{1,0:T(1,128)} %bitcast.10, ...), custom_call_target="tpu_custom_call" | custom-call | tf_op jit(solution)/shard_map/ader_updates/pallas_call | solution.py:601
  19.6 0.0 copy-done
  19.6 0.8 %select_live.1 = (f32[9,35,256]{2,1,0:T(8,128)}, f32[3,15,32]{2,1,0:T(8,128)}) custom-call(s32[1,128]{1,0:T(1,128)S(1)} %pad_bitcast_fusion.live, f32[9,35,256]{2,1,0:T(8,128)S(1)} %copy-done, f32[9,35,256]{2,1,0:T(8,128)S(1)} %get-tuple-element.4.updated, f32[3,15,32]{2,1,0:T(8,128)S(1)} %get-tuple-element.5.slip), custom_call_target="tpu_custom_call" | custom-call | tf_op jit(solution)/shard_map/select_live/pallas_call | solution.py:659
  (1 shorter events, 0.0 us)
Async XLA Ops:
  0.6 19.0 %copy-start = (f32[9,35,256]{2,1,0:T(8,128)S(1)}, f32[9,35,256]{2,1,0:T(8,128)}, u32[]{:S(2)}) copy-start(f32[9,35,256]{2,1,0:T(8,128)} %un.1) | copy-start | bytes 967684
